TPU v7x, 32 devices: a whole 2x2x4 slice. The times are simulated.
32 devices in a mesh: layer: 8 (over y, x, core), lat: 4 (over z).
Axes of the slice: x: 2, y: 2, z: 4, core: 2. Of those that a mesh axis runs over, the one named last changes fastest.
Arguments:
- inputs: bfloat16 [4, 128, 2048], P(None, None, 'lat'), may hold values from -6 to 6
- targets: bfloat16 [512, 2048], P(('layer', 'lat')), may hold values from -6 to 6
- top_index: int32 [4, 128, 64], replicated, may hold values from 0 to 8191, all different within a row
- enc_weight: bfloat16 [2048, 32768], P(None, ('layer', 'lat')), may hold values from -0.125 to 0.125
- dec_weight: bfloat16 [32768, 4, 2048], P(('layer', 'lat')), may hold values from -0.375 to 0.375
Outputs:
- errors: float32 [512, 2048], P(('layer', 'lat'))
- grad_enc: bfloat16 [2048, 32768], P(None, ('layer', 'lat'))
- grad_dec: bfloat16 [32768, 4, 2048], P(('layer', 'lat'))
Inputs may be any that keep to these rules, and one draw needn't show every extreme that they name: `top_index`: each row names 64 different latents.
All inputs are finite; a program needn't handle non-finite values.
Results may differ from a plain program's by a relative error of at most 0.009.
Values may be sent and summed in bfloat16 or wider, within the bound.
A program may use at most 128 MiB of HBM per device.

v0:
```python
import jax
import jax.numpy as jnp
from jax import lax
from jax.sharding import PartitionSpec as P


def per_device(inputs, targets, top_index, enc_weight, dec_weight):
    n_layer = lax.axis_size("layer")
    n_lat = lax.axis_size("lat")
    layer_count = inputs.shape[0]
    tok_count = inputs.shape[1]
    lat_dev = enc_weight.shape[1]
    per_layer = n_layer // layer_count
    layer_id = lax.axis_index("layer") // per_layer
    lat_first = (lax.axis_index("layer") % per_layer * n_lat + lax.axis_index("lat")) * lat_dev
    own_part = lax.dynamic_index_in_dim(inputs, layer_id, 0, keepdims=False)
    features = lax.all_gather(own_part, "lat", axis=1, tiled=True)
    preact = jnp.dot(features, enc_weight, preferred_element_type=jnp.float32)
    chosen = lax.dynamic_index_in_dim(top_index, layer_id, 0, keepdims=False)
    lat_ids = lat_first + jnp.arange(lat_dev, dtype=jnp.int32)
    active = jnp.any(chosen[:, :, None] == lat_ids[None, None, :], axis=1).astype(jnp.float32)
    code_vals = (preact * active).astype(jnp.bfloat16)
    reach_mask = (jnp.arange(layer_count, dtype=jnp.int32) >= layer_id).astype(jnp.float32)
    width = dec_weight.shape[2]
    row_count = targets.shape[0] * lax.axis_size(("layer", "lat"))
    result = jnp.einsum("nf,ftd->tnd", code_vals, dec_weight, preferred_element_type=jnp.float32)
    result = result * reach_mask[:, None, None]
    decoded = lax.psum_scatter(
        result.reshape(row_count, width), ("layer", "lat"), scatter_dimension=0, tiled=True
    )
    errors = decoded - targets.astype(jnp.float32)
    err_b = errors.astype(jnp.bfloat16)
    all_err = lax.all_gather(err_b, ("layer", "lat"), axis=0, tiled=True)
    err_used = (
        all_err.reshape(layer_count, tok_count, width)
        * reach_mask.astype(jnp.bfloat16)[:, None, None]
    )
    code_grad = jnp.einsum("lnd,fld->nf", err_used, dec_weight, preferred_element_type=jnp.float32)
    pre_grad = (code_grad * active).astype(jnp.bfloat16)
    grad_enc = lax.dot_general(
        features, pre_grad, (((0,), (0,)), ((), ())), preferred_element_type=jnp.float32
    ).astype(jnp.bfloat16)
    grad_dec = jnp.einsum(
        "nf,lnd->fld", code_vals, err_used, preferred_element_type=jnp.float32
    ).astype(jnp.bfloat16)
    return (errors, grad_enc, grad_dec)


def solution(mesh):
    in_specs = (
        P(None, None, "lat"),
        P(("layer", "lat"), None),
        P(),
        P(None, ("layer", "lat")),
        P(("layer", "lat"), None, None),
    )
    out_specs = (
        P(("layer", "lat"), None),
        P(None, ("layer", "lat")),
        P(("layer", "lat"), None, None),
    )
    return jax.shard_map(
        per_device, mesh=mesh, in_specs=in_specs, out_specs=out_specs, check_vma=False
    )
```

profile of v0, /device:TPU:0, one launch (start us, length us, event | category | flops | bytes accessed | tf_op | source)
XLA Modules:
  0.0 331.6 jit_solution(4044951903182924780)
XLA Ops:
  7.2 0.0 copy-start
  7.2 0.0 reduce-scatter.2.cloned.1.call-start
  7.3 0.9 copy-done
  8.2 17.4 %all-gather = bf16[1,128,2048]{2,1,0:T(8,128)(2,1)S(1)} all-gather(bf16[1,128,512]{2,1,0:T(8,128)(2,1)S(1)} %constant_dynamic-slice_fusion), channel_id=2, replica_groups=mesh['layer'=8,'lat'=4] {'lat'}, dimensions={2}, use_global_device_ids=true | all-gather | bytes 655360 | tf_op jit(solution)/shard_map/all_gather | solution.py:17
  25.6 0.8 dynamic-slice_bitcast_fusion
  26.3 0.1 copy.15
  26.5 4.7 %compare_reduce_fusion = pred[128,1024]{1,0:T(8,128)(4,1)S(1)} fusion(s32[1024]{0:T(1024)S(1)} %iota_add_fusion, s32[128,64]{1,0:T(8,128)S(1)} %copy.15), kind=kLoop, calls=%fused_computation | loop fusion | flops 16646144 | bytes 167936 | tf_op jit(solution)/shard_map/reduce_or | solution.py:21
  31.2 2.9 fusion.25
  34.1 26.9 %fusion.4 = f32[128,4,2048]{2,0,1:T(8,128)} fusion(bf16[128,1024,1]{1,0,2:T(8,128)(2,1)S(1)} %fusion.25, bf16[1024,4,2048]{2,1,0:T(4,128)(2,1)} %param.9, f32[4]{0:T(128)S(1)} %compare_convert_fusion), kind=kOutput, calls=%fused_computation.7 | convolution fusion | flops 2148532224 | bytes 21233680 | tf_op jit(solution)/shard_map/nf,ftd->tnd/dot_general | solution.py:26
  61.0 0.0 copy-start.3
  61.0 0.0 reduce-scatter.2.cloned.1.call-update
  61.0 0.0 all-gather.3.cloned.1.call-start
  61.1 149.8 %reduce-scatter.2.cloned.1.call-done = f32[16,2048]{1,0:T(8,128)} async-done(((f32[512,2048]{1,0:T(8,128)}), f32[16,2048]{1,0:T(8,128)}) %reduce-scatter.2.cloned.1.call-update) | async-done | bytes 131088 | tf_op jit(solution)/shard_map/reduce_scatter | solution.py:28
  210.9 0.0 copy-done.3
  210.9 1.6 fusion.31
  212.5 0.0 all-gather.3.cloned.1.call-update
  212.5 56.6 %all-gather.3.cloned.1.call-done = bf16[512,2048]{1,0:T(8,128)(2,1)} async-done(((bf16[16,2048]{1,0:T(8,128)(2,1)}), bf16[512,2048]{1,0:T(8,128)(2,1)}) %all-gather.3.cloned.1.call-update) | async-done | bytes 2097168 | tf_op jit(solution)/shard_map/all_gather | solution.py:33
  269.1 0.0 copy-start.2
  269.1 9.9 %convolution_convert_fusion = bf16[1024,4,2048]{2,0,1:T(8,128)(2,1)} fusion(bf16[128,1024,1]{1,0,2:T(8,128)(2,1)S(1)} %fusion.25, bf16[4,128,2048]{2,1,0:T(8,128)(2,1)} %bitcast.25, bf16[4]{0:T(256)(128)(2,1)S(1)} %fusion.30), kind=kOutput, calls=%fused_computation.5 | convolution fusion | flops 2160066560 | bytes 19136520 | tf_op jit(solution)/shard_map/nf,lnd->fld/dot_general | solution.py:43
  279.0 0.0 copy-done.2
  279.0 20.3 %fusion.20 = bf16[128,1024]{1,0:T(8,128)(2,1)S(1)} fusion(pred[128,1024]{1,0:T(8,128)(4,1)S(1)} %compare_reduce_fusion, bf16[1024,4,2048]{2,1,0:T(4,128)(2,1)} %param.9, bf16[4,128,2048]{2,1,0:T(8,128)(2,1)S(1)} %bitcast.26, bf16[4]{0:T(256)(128)(2,1)S(1)} %fusion.30), kind=kOutput, calls=%fused_computation.14 | convolution fusion | flops 2148794368 | bytes 19267592 | tf_op jit(solution)/shard_map/lnd,fld->nf/dot_general | solution.py:38
  299.3 0.0 copy-start.1
  299.3 22.2 %copy.19 = bf16[1024,4,2048]{2,1,0:T(4,128)(2,1)} copy(bf16[1024,4,2048]{2,0,1:T(8,128)(2,1)} %convolution_convert_fusion) | data formatting | bytes 33554432
  321.5 3.3 convolution_convert_fusion.1
  324.8 0.0 copy-done.1
  (4 shorter events, 0.0 us)
Async XLA Ops:
  7.2 1.1 copy-start
  7.2 203.7 %reduce-scatter.2.cloned.1.call-start = ((), (), s32[]{:S(2)}) async-start(), calls=%async_computation.1 | async-start | bytes 4325376 | tf_op jit(solution)/shard_map/reduce_scatter | solution.py:28
  61.0 149.9 %copy-start.3 = (bf16[16,2048]{1,0:T(8,128)(2,1)S(1)}, bf16[16,2048]{1,0:T(8,128)(2,1)}, u32[]{:S(2)}) copy-start(bf16[16,2048]{1,0:T(8,128)(2,1)} %param.6) | copy-start | bytes 196612
  61.0 208.1 %all-gather.3.cloned.1.call-start = ((), (), s32[]{:S(2)}) async-start(), calls=%async_computation.2 | async-start | bytes 2162688 | tf_op jit(solution)/shard_map/all_gather | solution.py:33
  269.1 9.9 %copy-start.2 = (bf16[512,2048]{1,0:T(8,128)(2,1)S(1)}, bf16[512,2048]{1,0:T(8,128)(2,1)}, u32[]{:S(2)}) copy-start(bf16[512,2048]{1,0:T(8,128)(2,1)} %all-gather.3.cloned.1.call-done) | copy-start | bytes 6291460
  299.3 25.5 %copy-start.1 = (bf16[4,128,512]{2,1,0:T(8,128)(2,1)S(1)}, bf16[4,128,512]{2,1,0:T(8,128)(2,1)}, u32[]{:S(2)}) copy-start(bf16[4,128,512]{2,1,0:T(8,128)(2,1)} %param.5) | copy-start | bytes 1572868
Sparse Core Ops, SparseCore 0:
  61.1 149.6 reduce-scatter.1
  214.4 54.6 all-gather.2
where the time goes:
time: 332 us
  waiting for transfers between devices  206 us (62%)
  matrix products  63.3 us (19%)
  local copies, waits for them, and re-layouts  24 us (7%)
  blocking collectives  17.4 us (5%)
  between operations  14.2 us (4%)
  other arithmetic  6.3 us (2%)
    reduce_scatter x1, waiting for transfers between devices, per_device(): lax.psum_scatter(result.reshape(row_count, width), ('layer', 'lat'), scat...  150 us
    all_gather x1, waiting for transfers between devices, per_device(): all_err = lax.all_gather(err_b, ('layer', 'lat'), axis=0, tiled=True)  56.6 us
    dot_general x1, matrix products, per_device(): jnp.einsum('nf,ftd->tnd', code_vals, dec_weight, preferred_element_type=j...  26.9 us
    unnamed x9, local copies, waits for them, and re-layouts  23.2 us
    dot_general x1, matrix products, per_device(): jnp.einsum('lnd,fld->nf', err_used, dec_weight, preferred_element_type=jn...  20.3 us
    all_gather x1, blocking collectives, per_device(): features = lax.all_gather(own_part, 'lat', axis=1, tiled=True)  17.4 us
    dot_general x1, matrix products, per_device(): jnp.einsum('nf,lnd->fld', code_vals, err_used, preferred_element_type=jnp...  9.86 us
  transfers between devices with their start and end apart: 2, of which 2 were waited for; matrix products, arithmetic and copies ran while one was open for 0% of the time, Pallas kernels for 0%

commit v1 on v0

--- a/solution.py
+++ b/solution.py
@@ -1,7 +1,223 @@
+import functools
+
 import jax
 import jax.numpy as jnp
 from jax import lax
+from jax.experimental import pallas as pl
+from jax.experimental.pallas import tpu as pltpu
 from jax.sharding import PartitionSpec as P
+
+BF = jnp.bfloat16
+F32 = jnp.float32
+CHUNKS = 2
+
+
+def exchange_kernel(n_t, n_lat, part, targets, errors, all_err,
+                    sib_rx, q, xy_rx, zs, z_rx,
+                    s1, r1, s2, r2, s3, r3, s4, r4, s5, r5, s6, r6):
+    row = lax.axis_index("layer")
+    z = lax.axis_index("lat")
+    s = row // 2
+    c = row % 2
+    width = part.shape[2]
+    half = part.shape[1] // 2
+    rows = half // n_lat
+    cw = width // CHUNKS
+    sibling = (s * 2 + 1 - c, z)
+    mine = pl.ds(pl.multiple_of(c * half, half), half)
+    other = pl.ds(pl.multiple_of((1 - c) * half, half), half)
+
+    def col(t):
+        return (2 * t + c, z)
+
+    def lat(zz):
+        return (row, zz)
+
+    def cols(ch):
+        return pl.ds(ch * cw, cw)
+
+    def rblock(zz):
+        return pl.ds(pl.multiple_of(zz * rows, rows), rows)
+
+    def eblock(zz):
+        return pl.ds(pl.multiple_of(c * half + zz * rows, rows), rows)
+
+    def copy(src, dst, ssem, rsem, dev):
+        return pltpu.make_async_remote_copy(
+            src_ref=src, dst_ref=dst, send_sem=ssem, recv_sem=rsem,
+            device_id=dev, device_id_type=pl.DeviceIdType.MESH)
+
+    barrier = pltpu.get_barrier_semaphore()
+    pl.semaphore_signal(barrier, inc=1, device_id=sibling, device_id_type=pl.DeviceIdType.MESH)
+    for t in range(n_t):
+        @pl.when(t != s)
+        def _():
+            pl.semaphore_signal(barrier, inc=1, device_id=col(t), device_id_type=pl.DeviceIdType.MESH)
+    for zz in range(n_lat):
+        @pl.when(zz != z)
+        def _():
+            pl.semaphore_signal(barrier, inc=1, device_id=lat(zz), device_id_type=pl.DeviceIdType.MESH)
+    pl.semaphore_wait(barrier, n_t + n_lat - 1)
+
+    def pair(ch, t):
+        return copy(part.at[t, other, cols(ch)], sib_rx.at[t, :, cols(ch)],
+                    s1.at[ch, t], r1.at[ch, t], sibling)
+
+    def to_target(ch, t):
+        return copy(q.at[t, :, cols(ch)], xy_rx.at[s, :, cols(ch)],
+                    s2.at[ch, t], r2.at[ch, s], col(t))
+
+    def from_source(ch, ss):
+        return copy(q.at[ss, :, cols(ch)], xy_rx.at[ss, :, cols(ch)],
+                    s2.at[ch, ss], r2.at[ch, ss], col(ss))
+
+    def to_lat(ch, zz):
+        return copy(zs.at[rblock(zz), cols(ch)], z_rx.at[z, :, cols(ch)],
+                    s3.at[ch, zz], r3.at[ch, z], lat(zz))
+
+    def from_lat(ch, zz):
+        return copy(zs.at[rblock(zz), cols(ch)], z_rx.at[zz, :, cols(ch)],
+                    s3.at[ch, zz], r3.at[ch, zz], lat(zz))
+
+    def err_to_lat(ch, zz):
+        return copy(all_err.at[s, eblock(z), cols(ch)], all_err.at[s, eblock(z), cols(ch)],
+                    s4.at[ch, zz], r4.at[ch, z], lat(zz))
+
+    def err_from_lat(ch, zz):
+        return copy(all_err.at[s, eblock(zz), cols(ch)], all_err.at[s, eblock(zz), cols(ch)],
+                    s4.at[ch, zz], r4.at[ch, zz], lat(zz))
+
+    def err_to_source(ch, ss):
+        return copy(all_err.at[s, mine, cols(ch)], all_err.at[s, mine, cols(ch)],
+                    s5.at[ch, ss], r5.at[ch, s], col(ss))
+
+    def err_from_target(ch, t):
+        return copy(all_err.at[t, mine, cols(ch)], all_err.at[t, mine, cols(ch)],
+                    s5.at[ch, t], r5.at[ch, t], col(t))
+
+    def err_pair(ch, t):
+        return copy(all_err.at[t, mine, cols(ch)], all_err.at[t, mine, cols(ch)],
+                    s6.at[ch, t], r6.at[ch, t], sibling)
+
+    def err_pair_in(ch, t):
+        return copy(all_err.at[t, other, cols(ch)], all_err.at[t, other, cols(ch)],
+                    s6.at[ch, t], r6.at[ch, t], sibling)
+
+    for ch in range(CHUNKS):
+        for t in reversed(range(n_t)):
+            @pl.when(t >= s)
+            def _():
+                pair(ch, t).start()
+    for t in range(n_t):
+        @pl.when(t < s)
+        def _():
+            all_err[t] = jnp.zeros((2 * half, width), BF)
+    for ch in range(CHUNKS):
+        for t in reversed(range(n_t)):
+            @pl.when(t >= s)
+            def _():
+                pair(ch, t).wait_recv()
+
+            @pl.when(t > s)
+            def _():
+                q[t, :, cols(ch)] = (part[t, mine, cols(ch)].astype(F32)
+                                     + sib_rx[t, :, cols(ch)].astype(F32)).astype(BF)
+                to_target(ch, t).start()
+    for ch in range(CHUNKS):
+        for ss in range(n_t):
+            @pl.when(ss == s)
+            def _():
+                total = (part[ss, mine, cols(ch)].astype(F32)
+                         + sib_rx[ss, :, cols(ch)].astype(F32))
+                for src in range(ss):
+                    from_source(ch, src).wait_recv()
+                    total = total + xy_rx[src, :, cols(ch)].astype(F32)
+                zs[:, cols(ch)] = total.astype(BF)
+        for zz in range(n_lat):
+            @pl.when(zz != z)
+            def _():
+                to_lat(ch, zz).start()
+    for ch in range(CHUNKS):
+        z_rx[z, :, cols(ch)] = zs[rblock(z), cols(ch)]
+        for zz in range(n_lat):
+            @pl.when(zz != z)
+            def _():
+                from_lat(ch, zz).wait_recv()
+        total = z_rx[0, :, cols(ch)].astype(F32)
+        for zz in range(1, n_lat):
+            total = total + z_rx[zz, :, cols(ch)].astype(F32)
+        err = total - targets[:, cols(ch)].astype(F32)
+        errors[:, cols(ch)] = err
+        all_err[s, eblock(z), cols(ch)] = err.astype(BF)
+        for zz in range(n_lat):
+            @pl.when(zz != z)
+            def _():
+                err_to_lat(ch, zz).start()
+    for ch in range(CHUNKS):
+        for zz in range(n_lat):
+            @pl.when(zz != z)
+            def _():
+                err_from_lat(ch, zz).wait_recv()
+        for ss in range(n_t):
+            @pl.when(ss < s)
+            def _():
+                err_to_source(ch, ss).start()
+        err_pair(ch, s).start()
+    for ch in range(CHUNKS):
+        for t in range(n_t):
+            @pl.when(t > s)
+            def _():
+                err_from_target(ch, t).wait_recv()
+                err_pair(ch, t).start()
+    for ch in range(CHUNKS):
+        for t in range(n_t):
+            @pl.when(t >= s)
+            def _():
+                err_pair_in(ch, t).wait_recv()
+                err_pair(ch, t).wait_send()
+                pair(ch, t).wait_send()
+
+            @pl.when(t > s)
+            def _():
+                to_target(ch, t).wait_send()
+
+            @pl.when(t < s)
+            def _():
+                err_to_source(ch, t).wait_send()
+        for zz in range(n_lat):
+            @pl.when(zz != z)
+            def _():
+                to_lat(ch, zz).wait_send()
+                err_to_lat(ch, zz).wait_send()
+
+
+def exchange(part, targets):
+    n_t, tok, width = part.shape
+    n_lat = lax.axis_size("lat")
+    half = tok // 2
+    rows = half // n_lat
+    vm = pl.BlockSpec(memory_space=pltpu.VMEM)
+    dma = pltpu.SemaphoreType.DMA
+    sems = []
+    for n in (n_t, n_t, n_lat, n_lat, n_t, n_t):
+        sems += [dma((CHUNKS, n)), dma((CHUNKS, n))]
+    return pl.pallas_call(
+        functools.partial(exchange_kernel, n_t, n_lat),
+        out_shape=(jax.ShapeDtypeStruct((rows, width), F32),
+                   jax.ShapeDtypeStruct((n_t, tok, width), BF)),
+        in_specs=[vm, vm],
+        out_specs=(vm, vm),
+        scratch_shapes=[
+            pltpu.VMEM((n_t, half, width), BF),
+            pltpu.VMEM((n_t, half, width), BF),
+            pltpu.VMEM((n_t, half, width), BF),
+            pltpu.VMEM((half, width), BF),
+            pltpu.VMEM((n_lat, rows, width), BF),
+        ] + sems,
+        compiler_params=pltpu.CompilerParams(
+            collective_id=0, has_side_effects=True, vmem_limit_bytes=24 * 2**20),
+        cost_estimate=pl.CostEstimate(flops=2**24, bytes_accessed=2**24, transcendentals=0),
+    )(part, targets)
 
 
 def per_device(inputs, targets, top_index, enc_weight, dec_weight):
@@ -24,17 +240,20 @@
     width = dec_weight.shape[2]
     row_count = targets.shape[0] * lax.axis_size(("layer", "lat"))
     result = jnp.einsum("nf,ftd->tnd", code_vals, dec_weight, preferred_element_type=jnp.float32)
-    result = result * reach_mask[:, None, None]
-    decoded = lax.psum_scatter(
-        result.reshape(row_count, width), ("layer", "lat"), scatter_dimension=0, tiled=True
-    )
-    errors = decoded - targets.astype(jnp.float32)
-    err_b = errors.astype(jnp.bfloat16)
-    all_err = lax.all_gather(err_b, ("layer", "lat"), axis=0, tiled=True)
-    err_used = (
-        all_err.reshape(layer_count, tok_count, width)
-        * reach_mask.astype(jnp.bfloat16)[:, None, None]
-    )
+    if per_layer == 2 and targets.shape[0] * 2 * n_lat == tok_count and targets.shape[0] % 16 == 0:
+        errors, err_used = exchange(result.astype(BF), targets)
+    else:
+        result = result * reach_mask[:, None, None]
+        decoded = lax.psum_scatter(
+            result.reshape(row_count, width), ("layer", "lat"), scatter_dimension=0, tiled=True
+        )
+        errors = decoded - targets.astype(jnp.float32)
+        err_b = errors.astype(jnp.bfloat16)
+        all_err = lax.all_gather(err_b, ("layer", "lat"), axis=0, tiled=True)
+        err_used = (
+            all_err.reshape(layer_count, tok_count, width)
+            * reach_mask.astype(jnp.bfloat16)[:, None, None]
+        )
     code_grad = jnp.einsum("lnd,fld->nf", err_used, dec_weight, preferred_element_type=jnp.float32)
     pre_grad = (code_grad * active).astype(jnp.bfloat16)
     grad_enc = lax.dot_general(

time: 332 us -> 148 us (0.45)
  waiting for transfers between devices: 206 us -> 0 us
  Pallas kernels: 0 us -> 39.3 us
  between operations: 14.2 us -> 0.76 us
    reduce_scatter x1 -> x0, waiting for transfers between devices: 150 us -> none  [per_device(): lax.psum_scatter(result.reshape(row_count, width), ('layer', 'lat'), scat...]
    all_gather x1 -> x0, waiting for transfers between devices: 56.6 us -> none  [per_device(): all_err = lax.all_gather(err_b, ('layer', 'lat'), axis=0, tiled=True)]
    pallas_call x0 -> x1, Pallas kernels: none -> 39.3 us  [exchange(): pl.pallas_call(functools.partial(exchange_kernel, n_t, n_lat), out_shape=...]
    unnamed x9 -> x10, local copies, waits for them, and re-layouts: 23.2 us -> 23.9 us
  transfers between devices with their start and end apart: 2 -> 0, of which waited for: 2 -> 0; matrix products, arithmetic and copies ran while one was open for 0% -> 0% of each run, Pallas kernels for 0% -> 0%
where the time goes in v1:
time: 148 us
  matrix products  61.1 us (41%)
  Pallas kernels  39.3 us (27%)
  local copies, waits for them, and re-layouts  24.7 us (17%)
  blocking collectives  17.4 us (12%)
  other arithmetic  4.7 us (3%)
    pallas_call x1, Pallas kernels, exchange(): pl.pallas_call(functools.partial(exchange_kernel, n_t, n_lat), out_shape=...  39.3 us
    dot_general x1, matrix products, per_device(): jnp.einsum('nf,ftd->tnd', code_vals, dec_weight, preferred_element_type=j...  24.8 us
    unnamed x10, local copies, waits for them, and re-layouts  23.9 us
    dot_general x1, matrix products, per_device(): jnp.einsum('lnd,fld->nf', err_used, dec_weight, preferred_element_type=jn...  20.7 us
    all_gather x1, blocking collectives, per_device(): features = lax.all_gather(own_part, 'lat', axis=1, tiled=True)  17.4 us
    dot_general x1, matrix products, per_device(): jnp.einsum('nf,lnd->fld', code_vals, err_used, preferred_element_type=jnp...  8.38 us
    reduce_or x1, other arithmetic, per_device(): jnp.any(chosen[:, :, None] == lat_ids[None, None, :], axis=1)  4.7 us
    dot_general x1, matrix products, per_device(): lax.dot_general(features, pre_grad, (((0,), (0,)), ((), ())), preferred_e...  4.24 us

profile of v1, /device:TPU:0, one launch (start us, length us, event | category | flops | bytes accessed | tf_op | source)
XLA Modules:
  0.0 147.9 jit_solution(17196058339663982296)
XLA Ops:
  0.6 0.0 copy-start
  0.7 1.0 copy-done
  1.7 17.4 %all-gather = bf16[1,128,2048]{2,1,0:T(8,128)(2,1)S(1)} all-gather(bf16[1,128,512]{2,1,0:T(8,128)(2,1)S(1)} %constant_dynamic-slice_fusion), channel_id=2, replica_groups=mesh['layer'=8,'lat'=4] {'lat'}, dimensions={2}, use_global_device_ids=true | all-gather | bytes 655360 | tf_op jit(solution)/shard_map/all_gather | solution.py:233
  19.0 0.8 dynamic-slice_bitcast_fusion
  19.8 0.1 copy.15
  19.9 4.7 %compare_reduce_fusion = pred[128,1024]{1,0:T(8,128)(4,1)S(1)} fusion(s32[1024]{0:T(1024)S(1)} %iota_add_fusion, s32[128,64]{1,0:T(8,128)S(1)} %copy.15), kind=kLoop, calls=%fused_computation | loop fusion | flops 16646144 | bytes 167936 | tf_op jit(solution)/shard_map/reduce_or | solution.py:237
  24.6 0.0 copy-start.2
  24.6 3.0 %fusion.20 = bf16[128,1024,1]{1,0,2:T(8,128)(2,1)S(1)} fusion(pred[128,1024]{1,0:T(8,128)(4,1)S(1)} %compare_reduce_fusion, bf16[2048,1024]{1,0:T(8,128)(2,1)} %param.8, bf16[1,128,2048]{2,1,0:T(8,128)(2,1)S(1)} %all-gather), kind=kOutput, calls=%fused_computation.14 | convolution fusion | flops 537133056 | bytes 5111808 | tf_op jit(solution)/shard_map/dot_general | solution.py:234
  27.6 0.0 copy-done.2
  27.6 0.0 copy-start.1
  27.6 24.8 %fusion.7.part = bf16[4,128,2048]{2,1,0:T(8,128)(2,1)S(1)} fusion(bf16[128,1024,1]{1,0,2:T(8,128)(2,1)S(1)} %fusion.20, bf16[1024,4,2048]{2,1,0:T(4,128)(2,1)} %param.9), kind=kOutput, calls=%fused_computation.8 | convolution fusion | flops 2148532224 | bytes 19136512 | tf_op jit(solution)/shard_map/nf,ftd->tnd/dot_general | solution.py:242
  52.5 0.0 copy-done.1
  52.5 39.3 %shard_map.76 = (f32[16,2048]{1,0:T(8,128)S(1)}, bf16[4,128,2048]{2,1,0:T(8,128)(2,1)S(1)}) custom-call(bf16[4,128,2048]{2,1,0:T(8,128)(2,1)S(1)} %fusion.7.part, bf16[16,2048]{1,0:T(8,128)(2,1)S(1)} %copy-done.1), custom_call_target="tpu_custom_call" | custom-call | flops 16777216 | bytes 16777216 | tf_op jit(solution)/shard_map/pallas_call | solution.py:204
  91.7 8.4 %convolution_convert_fusion = bf16[1024,4,2048]{2,0,1:T(8,128)(2,1)} fusion(bf16[128,1024,1]{1,0,2:T(8,128)(2,1)S(1)} %fusion.20, bf16[4,128,2048]{2,1,0:T(8,128)(2,1)S(1)} %get-tuple-element.6), kind=kOutput, calls=%fused_computation.5 | convolution fusion | flops 2155872256 | bytes 19136512 | tf_op jit(solution)/shard_map/nf,lnd->fld/dot_general | solution.py:262
  100.1 0.0 copy-start.3
  100.1 22.2 %copy.19 = bf16[1024,4,2048]{2,1,0:T(4,128)(2,1)} copy(bf16[1024,4,2048]{2,0,1:T(8,128)(2,1)} %convolution_convert_fusion) | data formatting | bytes 33554432
  122.3 0.0 copy-done.3
  122.3 20.7 %fusion.17 = bf16[128,1024]{1,0:T(8,128)(2,1)} fusion(pred[128,1024]{1,0:T(8,128)(4,1)S(1)} %copy-done.3, bf16[4,128,2048]{2,1,0:T(8,128)(2,1)S(1)} %get-tuple-element.6, bf16[1024,4,2048]{2,1,0:T(4,128)(2,1)} %param.9), kind=kOutput, calls=%fused_computation.13 | convolution fusion | flops 2147745792 | bytes 19267584 | tf_op jit(solution)/shard_map/lnd,fld->nf/dot_general | solution.py:257
  143.0 4.2 %convolution_convert_fusion.1 = bf16[2048,1024]{1,0:T(8,128)(2,1)} fusion(bf16[128,1024]{1,0:T(8,128)(2,1)} %fusion.17, bf16[1,128,2048]{2,1,0:T(8,128)(2,1)S(1)} %all-gather), kind=kOutput, calls=%fused_computation.6 | convolution fusion | flops 538968064 | bytes 4980736 | tf_op jit(solution)/shard_map/dot_general | solution.py:259
  147.3 0.7 copy.37
  (2 shorter events, 0.0 us)
Async XLA Ops:
  0.6 1.0 copy-start
  24.6 3.0 %copy-start.2 = (pred[128,1024]{1,0:T(8,128)(4,1)}, pred[128,1024]{1,0:T(8,128)(4,1)S(1)}, u32[]{:S(2)}) copy-start(pred[128,1024]{1,0:T(8,128)(4,1)S(1)} %compare_reduce_fusion) | copy-start | bytes 393220
  27.6 24.9 %copy-start.1 = (bf16[16,2048]{1,0:T(8,128)(2,1)S(1)}, bf16[16,2048]{1,0:T(8,128)(2,1)}, u32[]{:S(2)}) copy-start(bf16[16,2048]{1,0:T(8,128)(2,1)} %targets.1) | copy-start | bytes 196612
  100.1 22.2 %copy-start.3 = (pred[128,1024]{1,0:T(8,128)(4,1)S(1)}, pred[128,1024]{1,0:T(8,128)(4,1)}, u32[]{:S(2)}) copy-start(pred[128,1024]{1,0:T(8,128)(4,1)} %copy-done.2) | copy-start | bytes 393220

commit v2 on v1

--- a/solution.py
+++ b/solution.py
@@ -220,6 +220,261 @@
     )(part, targets)
 
 
+def gather_kernel(n_lat, own, feat, s1, r1, s2, r2):
+    row = lax.axis_index("layer")
+    z = lax.axis_index("lat")
+    s = row // 2
+    c = row % 2
+    cut = own.shape[2]
+    piece = cut // 2
+    sibling = (s * 2 + 1 - c, z)
+    mesh_id = pl.DeviceIdType.MESH
+
+    def cols(zz, cc):
+        return pl.ds(pl.multiple_of(zz * cut + cc * piece, piece), piece)
+
+    barrier = pltpu.get_barrier_semaphore()
+    pl.semaphore_signal(barrier, inc=1, device_id=sibling, device_id_type=mesh_id)
+    for zz in range(n_lat):
+        @pl.when(zz != z)
+        def _():
+            pl.semaphore_signal(barrier, inc=1, device_id=(row, zz), device_id_type=mesh_id)
+    pl.semaphore_wait(barrier, n_lat)
+
+    def send(zz):
+        return pltpu.make_async_remote_copy(
+            src_ref=own.at[s, :, pl.ds(pl.multiple_of(c * piece, piece), piece)],
+            dst_ref=feat.at[:, cols(z, c)], send_sem=s1.at[zz], recv_sem=r1.at[z],
+            device_id=(row, zz), device_id_type=mesh_id)
+
+    def arrive(zz):
+        return pltpu.make_async_remote_copy(
+            src_ref=feat.at[:, cols(zz, c)],
+            dst_ref=feat.at[:, cols(zz, c)], send_sem=s1.at[zz], recv_sem=r1.at[zz],
+            device_id=(row, zz), device_id_type=mesh_id)
+
+    def forward(zz, cc):
+        return pltpu.make_async_remote_copy(
+            src_ref=feat.at[:, cols(zz, cc)],
+            dst_ref=feat.at[:, cols(zz, cc)], send_sem=s2.at[zz], recv_sem=r2.at[zz],
+            device_id=sibling, device_id_type=mesh_id)
+
+    for zz in range(n_lat):
+        @pl.when(zz != z)
+        def _():
+            send(zz).start()
+    feat[:, pl.ds(pl.multiple_of(z * cut, cut), cut)] = own[s]
+    for zz in range(n_lat):
+        @pl.when(zz != z)
+        def _():
+            arrive(zz).wait_recv()
+            forward(zz, c).start()
+    for zz in range(n_lat):
+        @pl.when(zz != z)
+        def _():
+            forward(zz, 1 - c).wait_recv()
+            forward(zz, c).wait_send()
+            send(zz).wait_send()
+
+
+def gather_features(inputs):
+    n_lat = lax.axis_size("lat")
+    _, tok, cut = inputs.shape
+    vm = pl.BlockSpec(memory_space=pltpu.VMEM)
+    dma = pltpu.SemaphoreType.DMA((n_lat,))
+    return pl.pallas_call(
+        functools.partial(gather_kernel, n_lat),
+        out_shape=jax.ShapeDtypeStruct((tok, cut * n_lat), BF),
+        in_specs=[vm],
+        out_specs=vm,
+        scratch_shapes=[dma, dma, dma, dma],
+        compiler_params=pltpu.CompilerParams(
+            collective_id=1, has_side_effects=True, vmem_limit_bytes=4 * 2**20),
+        cost_estimate=pl.CostEstimate(flops=2**20, bytes_accessed=2**21, transcendentals=0),
+    )(inputs)
+
+
+def spread_matrix(fb, n_t):
+    f = lax.broadcasted_iota(jnp.int32, (fb, fb * n_t), 0)
+    q = lax.broadcasted_iota(jnp.int32, (fb, fb * n_t), 1)
+    return ((q >= f * n_t) & (q < (f + 1) * n_t)).astype(F32).astype(BF)
+
+
+def load_copies(dec, xin, sem, block, fb):
+    rows = pl.ds(block * fb, fb)
+    return [pltpu.make_async_copy(dec.at[rows, :, pl.ds(j * 128, 128)],
+                                  xin.at[j, rows], sem.at[block, j])
+            for j in range(xin.shape[0])]
+
+
+def wide(ref, first, count, block, fb):
+    n_t = ref.shape[2]
+    parts = [ref.at[first + j, pl.ds(block * fb, fb)].reshape(fb * n_t, 128)[...]
+             for j in range(count)]
+    return jnp.concatenate(parts, axis=1)
+
+
+GROUP = 4
+
+
+def decode_kernel(fb, n_blocks, feat, chosen, ids, enc, dec, part, codes, active,
+                  xin, acc, lhs, spread, sem):
+    n_t, tok, width = part.shape
+    for b in range(n_blocks):
+        for cp in load_copies(dec, xin, sem, b, fb):
+            cp.start()
+    spread[...] = spread_matrix(fb, n_t)
+    target = lax.broadcasted_iota(jnp.int32, (tok, fb * n_t), 1) % n_t
+    for b in range(n_blocks):
+        cols = pl.ds(b * fb, fb)
+        lat = ids[:, cols]
+        chosen_b = chosen[...]
+        hit = jnp.zeros((tok, fb), jnp.bool_)
+        for k in range(chosen_b.shape[1]):
+            hit = hit | (chosen_b[:, k:k + 1] == lat)
+        on = hit.astype(F32)
+        active[:, cols] = on
+        pre = jnp.dot(feat[...], enc[:, cols], preferred_element_type=F32)
+        code = (pre * on).astype(BF)
+        codes[:, cols] = code
+        rep = jnp.dot(code, spread[...], preferred_element_type=F32)
+        for t in range(n_t):
+            lhs[t * tok:(t + 1) * tok, :] = jnp.where(target == t, rep, 0.0).astype(BF)
+        for cp in load_copies(dec, xin, sem, b, fb):
+            cp.wait()
+
+        @pl.loop(0, width // (128 * GROUP))
+        def _(g):
+            at = pl.ds(pl.multiple_of(g * 128 * GROUP, 128 * GROUP), 128 * GROUP)
+            out = jnp.dot(lhs[...], wide(xin, g * GROUP, GROUP, b, fb),
+                          preferred_element_type=F32)
+            if b > 0:
+                out = out + acc[:, at]
+            if b < n_blocks - 1:
+                acc[:, at] = out
+            else:
+                part[:, :, at] = out.astype(BF).reshape(n_t, tok, 128 * GROUP)
+
+
+def decode(features, chosen, ids, enc, dec):
+    lat_dev, n_t, width = dec.shape
+    tok = features.shape[0]
+    fb = 256
+    n_blocks = lat_dev // fb
+    vm = pl.BlockSpec(memory_space=pltpu.VMEM)
+    return pl.pallas_call(
+        functools.partial(decode_kernel, fb, n_blocks),
+        out_shape=(jax.ShapeDtypeStruct((n_t, tok, width), BF),
+                   jax.ShapeDtypeStruct((tok, lat_dev), BF),
+                   jax.ShapeDtypeStruct((tok, lat_dev), F32)),
+        in_specs=[vm, vm, vm, vm, pl.BlockSpec(memory_space=pl.ANY)],
+        out_specs=(vm, vm, vm),
+        scratch_shapes=[
+            pltpu.VMEM((width // 128, lat_dev, n_t, 128), BF),
+            pltpu.VMEM((n_t * tok, width), F32),
+            pltpu.VMEM((n_t * tok, fb * n_t), BF),
+            pltpu.VMEM((fb, fb * n_t), BF),
+            pltpu.SemaphoreType.DMA((n_blocks, width // 128)),
+        ],
+        compiler_params=pltpu.CompilerParams(vmem_limit_bytes=52 * 2**20),
+        cost_estimate=pl.CostEstimate(
+            flops=10 * 10**9, bytes_accessed=2**24 + 2**22, transcendentals=0),
+    )(features, chosen, ids, enc, dec)
+
+
+def grad_kernel(fb, n_blocks, feat, codes, active, err, dec, grad_enc, grad_dec,
+                xin, yout, gsum, lhs, spread, ebuf, sem, osem, esem):
+    tok = feat.shape[0]
+    rows_all, width = err.shape
+    n_t = rows_all // tok
+    for b in range(n_blocks):
+        for cp in load_copies(dec, xin, sem, b, fb):
+            cp.start()
+    spread[...] = spread_matrix(fb, n_t)
+    row_t = lax.broadcasted_iota(jnp.int32, (fb * n_t, tok), 0) % n_t
+    col_t = lax.broadcasted_iota(jnp.int32, (tok, fb * n_t), 1) % n_t
+    nt = (((1,), (1,)), ((), ()))
+    cw = 128 * GROUP
+    outs = []
+    for b in range(n_blocks):
+        cols = pl.ds(b * fb, fb)
+        rep = lax.dot_general(spread[...], codes[:, cols], (((0,), (1,)), ((), ())),
+                              preferred_element_type=F32)
+        for t in range(n_t):
+            lhs[:, t * tok:(t + 1) * tok] = jnp.where(row_t == t, rep, 0.0).astype(BF)
+
+        @pl.loop(0, width // cw)
+        def _(g):
+            at = pl.ds(pl.multiple_of(g * cw, cw), cw)
+            out = jnp.dot(lhs[...], err[:, at], preferred_element_type=F32).astype(BF)
+            for j in range(GROUP):
+                yout.at[g * GROUP + j, cols].reshape(fb * n_t, 128)[...] = (
+                    out[:, j * 128:(j + 1) * 128])
+
+        for j in range(width // 128):
+            cp = pltpu.make_async_copy(yout.at[j, cols],
+                                       grad_dec.at[cols, :, pl.ds(j * 128, 128)],
+                                       osem.at[b, j])
+            cp.start()
+            outs.append(cp)
+        for cp in load_copies(dec, xin, sem, b, fb):
+            cp.wait()
+        gsum[...] = jnp.zeros_like(gsum)
+
+        @pl.loop(0, width // cw)
+        def _(g):
+            at = pl.ds(pl.multiple_of(g * cw, cw), cw)
+            gsum[...] += lax.dot_general(err[:, at], wide(xin, g * GROUP, GROUP, b, fb), nt,
+                                         preferred_element_type=F32)
+
+        own = jnp.zeros((tok, fb * n_t), F32)
+        for t in range(n_t):
+            own = jnp.where(col_t == t, gsum[t * tok:(t + 1) * tok, :], own)
+        high = own.astype(BF)
+        low = (own - high.astype(F32)).astype(BF)
+        code_grad = (lax.dot_general(high, spread[...], nt, preferred_element_type=F32)
+                     + lax.dot_general(low, spread[...], nt, preferred_element_type=F32))
+        pre_grad = (code_grad * active[:, cols]).astype(BF)
+        ebuf[:, cols] = lax.dot_general(
+            feat[...], pre_grad, (((0,), (0,)), ((), ())), preferred_element_type=F32
+        ).astype(BF)
+        cp = pltpu.make_async_copy(ebuf.at[:, cols], grad_enc.at[:, cols], esem.at[b])
+        cp.start()
+        outs.append(cp)
+    for cp in outs:
+        cp.wait()
+
+
+def grads(features, codes, active, err, dec):
+    lat_dev, n_t, width = dec.shape
+    tok, d_in = features.shape
+    fb = 256
+    n_blocks = lat_dev // fb
+    vm = pl.BlockSpec(memory_space=pltpu.VMEM)
+    hbm = pl.BlockSpec(memory_space=pl.ANY)
+    tiles = pltpu.VMEM((width // 128, lat_dev, n_t, 128), BF)
+    return pl.pallas_call(
+        functools.partial(grad_kernel, fb, n_blocks),
+        out_shape=(jax.ShapeDtypeStruct((d_in, lat_dev), BF),
+                   jax.ShapeDtypeStruct((lat_dev, n_t, width), BF)),
+        in_specs=[vm, vm, vm, vm, hbm],
+        out_specs=(hbm, hbm),
+        scratch_shapes=[
+            tiles, tiles,
+            pltpu.VMEM((n_t * tok, fb * n_t), F32),
+            pltpu.VMEM((fb * n_t, n_t * tok), BF),
+            pltpu.VMEM((fb, fb * n_t), BF),
+            pltpu.VMEM((d_in, lat_dev), BF),
+            pltpu.SemaphoreType.DMA((n_blocks, width // 128)),
+            pltpu.SemaphoreType.DMA((n_blocks, width // 128)),
+            pltpu.SemaphoreType.DMA((n_blocks,)),
+        ],
+        compiler_params=pltpu.CompilerParams(vmem_limit_bytes=58 * 2**20),
+        cost_estimate=pl.CostEstimate(
+            flops=18 * 10**9, bytes_accessed=2**25 + 2**22, transcendentals=0),
+    )(features, codes, active, err, dec)
+
+
 def per_device(inputs, targets, top_index, enc_weight, dec_weight):
     n_layer = lax.axis_size("layer")
     n_lat = lax.axis_size("lat")
@@ -229,6 +484,18 @@
     per_layer = n_layer // layer_count
     layer_id = lax.axis_index("layer") // per_layer
     lat_first = (lax.axis_index("layer") % per_layer * n_lat + lax.axis_index("lat")) * lat_dev
+    tuned = (per_layer == 2 and layer_count == 4 and lat_dev % 256 == 0
+             and targets.shape[0] * 2 * n_lat == tok_count and targets.shape[0] % 16 == 0
+             and inputs.shape[2] % 256 == 0 and dec_weight.shape[2] % 512 == 0)
+    if tuned:
+        features = gather_features(inputs)
+        chosen = lax.dynamic_index_in_dim(top_index, layer_id, 0, keepdims=False)
+        ids = (lat_first + jnp.arange(lat_dev, dtype=jnp.int32))[None, :]
+        part, codes, active = decode(features, chosen, ids, enc_weight, dec_weight)
+        errors, err_used = exchange(part, targets)
+        grad_enc, grad_dec = grads(
+            features, codes, active, err_used.reshape(-1, err_used.shape[2]), dec_weight)
+        return (errors, grad_enc, grad_dec)
     own_part = lax.dynamic_index_in_dim(inputs, layer_id, 0, keepdims=False)
     features = lax.all_gather(own_part, "lat", axis=1, tiled=True)
     preact = jnp.dot(features, enc_weight, preferred_element_type=jnp.float32)
@@ -240,20 +507,17 @@
     width = dec_weight.shape[2]
     row_count = targets.shape[0] * lax.axis_size(("layer", "lat"))
     result = jnp.einsum("nf,ftd->tnd", code_vals, dec_weight, preferred_element_type=jnp.float32)
-    if per_layer == 2 and targets.shape[0] * 2 * n_lat == tok_count and targets.shape[0] % 16 == 0:
-        errors, err_used = exchange(result.astype(BF), targets)
-    else:
-        result = result * reach_mask[:, None, None]
-        decoded = lax.psum_scatter(
-            result.reshape(row_count, width), ("layer", "lat"), scatter_dimension=0, tiled=True
-        )
-        errors = decoded - targets.astype(jnp.float32)
-        err_b = errors.astype(jnp.bfloat16)
-        all_err = lax.all_gather(err_b, ("layer", "lat"), axis=0, tiled=True)
-        err_used = (
-            all_err.reshape(layer_count, tok_count, width)
-            * reach_mask.astype(jnp.bfloat16)[:, None, None]
-        )
+    result = result * reach_mask[:, None, None]
+    decoded = lax.psum_scatter(
+        result.reshape(row_count, width), ("layer", "lat"), scatter_dimension=0, tiled=True
+    )
+    errors = decoded - targets.astype(jnp.float32)
+    err_b = errors.astype(jnp.bfloat16)
+    all_err = lax.all_gather(err_b, ("layer", "lat"), axis=0, tiled=True)
+    err_used = (
+        all_err.reshape(layer_count, tok_count, width)
+        * reach_mask.astype(jnp.bfloat16)[:, None, None]
+    )
     code_grad = jnp.einsum("lnd,fld->nf", err_used, dec_weight, preferred_element_type=jnp.float32)
     pre_grad = (code_grad * active).astype(jnp.bfloat16)
     grad_enc = lax.dot_general(

time: 148 us -> 120 us (0.81)
  Pallas kernels: 39.3 us -> 112 us
  matrix products: 61.1 us -> 0 us
  local copies, waits for them, and re-layouts: 24.7 us -> 6.47 us
  blocking collectives: 17.4 us -> 0 us
  other arithmetic: 4.7 us -> 0.01 us
    pallas_call x0 -> x3, Pallas kernels: none -> 73.2 us  [the longest x1 36.2 us: grads(): pl.pallas_call(functools.partial(grad_kernel, fb, n_blocks), out_shape=(j...]
    dot_general x5 -> x0, matrix products: 61.1 us -> none  [the longest x1 24.8 us: per_device(): jnp.einsum('nf,ftd->tnd', code_vals, dec_weight, preferred_element_type=j...]
    unnamed x10 -> x17, local copies, waits for them, and re-layouts: 23.9 us -> 6.37 us
    all_gather x1 -> x0, blocking collectives: 17.4 us -> none  [per_device(): features = lax.all_gather(own_part, 'lat', axis=1, tiled=True)]
    reduce_or x1 -> x0, other arithmetic: 4.7 us -> none  [per_device(): jnp.any(chosen[:, :, None] == lat_ids[None, None, :], axis=1)]
where the time goes in v2:
time: 120 us; the launch traced here: 119 us
  Pallas kernels  112 us (93%)
  local copies, waits for them, and re-layouts  6.47 us (5%)
    pallas_call x1, Pallas kernels, exchange(): pl.pallas_call(functools.partial(exchange_kernel, n_t, n_lat), out_shape=...  38.9 us
    pallas_call x1, Pallas kernels, grads(): pl.pallas_call(functools.partial(grad_kernel, fb, n_blocks), out_shape=(j...  36.2 us
    pallas_call x1, Pallas kernels, decode(): pl.pallas_call(functools.partial(decode_kernel, fb, n_blocks), out_shape=...  25.1 us
    pallas_call x1, Pallas kernels, gather_features(): pl.pallas_call(functools.partial(gather_kernel, n_lat), out_shape=jax.Sha...  11.9 us
    unnamed x17, local copies, waits for them, and re-layouts  6.37 us

profile of v2, /device:TPU:0, one launch (start us, length us, event | category | flops | bytes accessed | tf_op | source)
XLA Modules:
  0.0 119.3 jit_solution(12436188703785095034)
XLA Ops:
  0.6 0.0 copy-start
  0.7 0.9 copy-done
  1.5 0.1 copy.8
  1.6 0.0 copy-start.2
  1.7 1.0 copy-done.2
  2.7 11.9 %shard_map.76.feat = bf16[128,2048]{1,0:T(8,128)(2,1)S(1)} custom-call(bf16[4,128,512]{2,1,0:T(8,128)(2,1)S(1)} %copy-done.2), custom_call_target="tpu_custom_call" | custom-call | flops 1048576 | bytes 2097152 | tf_op jit(solution)/shard_map/pallas_call | solution.py:285
  14.6 0.0 copy-start.3
  14.6 0.0 copy-start.4
  14.6 25.1 %shard_map.77 = (bf16[4,128,2048]{2,1,0:T(8,128)(2,1)}, bf16[128,1024]{1,0:T(8,128)(2,1)S(1)}, f32[128,1024]{1,0:T(8,128)S(1)}) custom-call(bf16[128,2048]{1,0:T(8,128)(2,1)S(1)} %shard_map.76.feat, s32[128,64]{1,0:T(8,128)S(1)} %bitcast.2, s32[1,1024]{1,0:T(1,128)S(1)} %iota_add_fusion.ids, bf16[2048,1024]{1,0:T(8,128)(2,1)} %enc.1, bf16[1024,4,2048]{2,1,0:T(4,128)(2,1)} %dec.3), custom_call_target="tpu_custom_call" | custom-call | flops 10000000000 | bytes 20971520 | tf_op jit(solution)/shard_map/pallas_call | solution.py:365
  39.7 0.0 copy-done.3
  39.7 0.0 copy-start.7
  39.7 0.7 copy-done.7
  40.4 0.0 copy-start.6
  40.4 0.0 copy-done.4
  40.4 0.0 copy-start.1
  40.4 1.8 %copy-done.1 = bf16[4,128,2048]{2,1,0:T(8,128)(2,1)S(1)} copy-done((bf16[4,128,2048]{2,1,0:T(8,128)(2,1)S(1)}, bf16[4,128,2048]{2,1,0:T(8,128)(2,1)}, u32[]{:S(2)}) %copy-start.1) | copy-done | bytes 2097176
  42.2 38.9 %shard_map.78 = (f32[16,2048]{1,0:T(8,128)S(1)}, bf16[4,128,2048]{2,1,0:T(8,128)(2,1)S(1)}) custom-call(bf16[4,128,2048]{2,1,0:T(8,128)(2,1)S(1)} %copy-done.1, bf16[16,2048]{1,0:T(8,128)(2,1)S(1)} %copy-done.4), custom_call_target="tpu_custom_call" | custom-call | flops 16777216 | bytes 16777216 | tf_op jit(solution)/shard_map/pallas_call | solution.py:204
  81.1 0.0 copy-done.6
  81.1 0.0 copy-start.5
  81.1 1.3 %copy-done.5 = bf16[4,128,2048]{2,1,0:T(8,128)(2,1)} copy-done((bf16[4,128,2048]{2,1,0:T(8,128)(2,1)}, bf16[4,128,2048]{2,1,0:T(8,128)(2,1)S(1)}, u32[]{:S(2)}) %copy-start.5) | copy-done | bytes 2097176
  82.4 36.2 %shard_map.79 = (bf16[2048,1024]{1,0:T(8,128)(2,1)}, bf16[1024,4,2048]{2,1,0:T(4,128)(2,1)}) custom-call(bf16[128,2048]{1,0:T(8,128)(2,1)} %copy-done.3, bf16[128,1024]{1,0:T(8,128)(2,1)} %copy-done.7, f32[128,1024]{1,0:T(8,128)} %copy-done.6, bf16[512,2048]{1,0:T(8,128)(2,1)} %bitcast.3, bf16[1024,4,2048]{2,1,0:T(4,128)(2,1)} %dec.3), custom_call_target="tpu_custom_call" | custom-call | flops 17999998976 | bytes 37748736 | tf_op jit(solution)/shard_map/pallas_call | solution.py:456
  118.7 0.7 copy.10
  (2 shorter events, 0.0 us)
Async XLA Ops:
  0.6 0.9 copy-start
  1.6 1.0 copy-start.2
  14.6 25.1 %copy-start.3 = (bf16[128,2048]{1,0:T(8,128)(2,1)}, bf16[128,2048]{1,0:T(8,128)(2,1)S(1)}, u32[]{:S(2)}) copy-start(bf16[128,2048]{1,0:T(8,128)(2,1)S(1)} %shard_map.76.feat) | copy-start | bytes 1572868
  14.6 25.8 %copy-start.4 = (bf16[16,2048]{1,0:T(8,128)(2,1)S(1)}, bf16[16,2048]{1,0:T(8,128)(2,1)}, u32[]{:S(2)}) copy-start(bf16[16,2048]{1,0:T(8,128)(2,1)} %targets.1) | copy-start | bytes 196612
  39.7 0.7 copy-start.7
  40.4 40.7 %copy-start.6 = (f32[128,1024]{1,0:T(8,128)}, f32[128,1024]{1,0:T(8,128)S(1)}, u32[]{:S(2)}) copy-start(f32[128,1024]{1,0:T(8,128)S(1)} %get-tuple-element.13.active) | copy-start | bytes 1572868
  40.4 1.8 %copy-start.1 = (bf16[4,128,2048]{2,1,0:T(8,128)(2,1)S(1)}, bf16[4,128,2048]{2,1,0:T(8,128)(2,1)}, u32[]{:S(2)}) copy-start(bf16[4,128,2048]{2,1,0:T(8,128)(2,1)} %get-tuple-element.10.part) | copy-start | bytes 6291460
  81.1 1.3 %copy-start.5 = (bf16[4,128,2048]{2,1,0:T(8,128)(2,1)}, bf16[4,128,2048]{2,1,0:T(8,128)(2,1)S(1)}, u32[]{:S(2)}) copy-start(bf16[4,128,2048]{2,1,0:T(8,128)(2,1)S(1)} %get-tuple-element.14) | copy-start | bytes 6291460

commit v3 on v1

--- a/solution.py
+++ b/solution.py
@@ -9,12 +9,35 @@
 
 BF = jnp.bfloat16
 F32 = jnp.float32
-CHUNKS = 2
-
-
-def exchange_kernel(n_t, n_lat, part, targets, errors, all_err,
-                    sib_rx, q, xy_rx, zs, z_rx,
-                    s1, r1, s2, r2, s3, r3, s4, r4, s5, r5, s6, r6):
+
+
+def spread_matrix(fb, n_t):
+    f = lax.broadcasted_iota(jnp.int32, (fb, fb * n_t), 0)
+    q = lax.broadcasted_iota(jnp.int32, (fb, fb * n_t), 1)
+    return ((q >= f * n_t) & (q < (f + 1) * n_t)).astype(F32).astype(BF)
+
+
+def load_copies(dec, xin, sem, block, fb):
+    rows = pl.ds(block * fb, fb)
+    return [pltpu.make_async_copy(dec.at[rows, :, pl.ds(j * 128, 128)],
+                                  xin.at[j, rows], sem.at[block, j])
+            for j in range(xin.shape[0])]
+
+
+def wide(ref, first, count, block, fb):
+    n_t = ref.shape[2]
+    parts = [ref.at[first + j, pl.ds(block * fb, fb)].reshape(fb * n_t, 128)[...]
+             for j in range(count)]
+    return jnp.concatenate(parts, axis=1)
+
+
+GROUP = 4
+
+
+def forward_kernel(n_t, n_lat, own, targets, chosen, ids, enc, dec,
+                   errors, all_err, feat, codes, active,
+                   xin, lhs, spread, acc, part, sib_rx, q, xy_rx, zs, z_rx, load_sem,
+                   s1, r1, s2, r2, s3, r3, s4, r4, s5, r5, s6, r6, s7, r7, s8, r8):
     row = lax.axis_index("layer")
     z = lax.axis_index("lat")
     s = row // 2
@@ -22,7 +45,12 @@
     width = part.shape[2]
     half = part.shape[1] // 2
     rows = half // n_lat
-    cw = width // CHUNKS
+    cw = 128 * GROUP
+    chunks = width // cw
+    fb = spread.shape[0]
+    n_blocks = codes.shape[1] // fb
+    cut = own.shape[2]
+    piece = cut // 2
     sibling = (s * 2 + 1 - c, z)
     mine = pl.ds(pl.multiple_of(c * half, half), half)
     other = pl.ds(pl.multiple_of((1 - c) * half, half), half)
@@ -47,6 +75,11 @@
             src_ref=src, dst_ref=dst, send_sem=ssem, recv_sem=rsem,
             device_id=dev, device_id_type=pl.DeviceIdType.MESH)
 
+    loads = [pltpu.make_async_copy(dec.at[:, :, pl.ds(j * 128, 128)], xin.at[j], load_sem.at[j])
+             for j in range(width // 128)]
+    for cp in loads:
+        cp.start()
+
     barrier = pltpu.get_barrier_semaphore()
     pl.semaphore_signal(barrier, inc=1, device_id=sibling, device_id_type=pl.DeviceIdType.MESH)
     for t in range(n_t):
@@ -103,16 +136,83 @@
         return copy(all_err.at[t, other, cols(ch)], all_err.at[t, other, cols(ch)],
                     s6.at[ch, t], r6.at[ch, t], sibling)
 
-    for ch in range(CHUNKS):
+    def fcols(zz, cc):
+        return pl.ds(pl.multiple_of(zz * cut + cc * piece, piece), piece)
+
+    def send(zz):
+        return copy(own.at[s, :, pl.ds(pl.multiple_of(c * piece, piece), piece)],
+                    feat.at[:, fcols(z, c)], s7.at[zz], r7.at[z], lat(zz))
+
+    def arrive(zz):
+        return copy(feat.at[:, fcols(zz, c)], feat.at[:, fcols(zz, c)],
+                    s7.at[zz], r7.at[zz], lat(zz))
+
+    def forward(zz, cc):
+        return copy(feat.at[:, fcols(zz, cc)], feat.at[:, fcols(zz, cc)],
+                    s8.at[zz], r8.at[zz], sibling)
+
+    for zz in range(n_lat):
+        @pl.when(zz != z)
+        def _():
+            send(zz).start()
+    feat[:, pl.ds(pl.multiple_of(z * cut, cut), cut)] = own[s]
+    for t in range(n_t):
+        @pl.when(t < s)
+        def _():
+            all_err[t] = jnp.zeros((2 * half, width), BF)
+    tok = 2 * half
+    spread[...] = spread_matrix(fb, n_t)
+    target = lax.broadcasted_iota(jnp.int32, (tok, fb * n_t), 1) % n_t
+
+    @pl.loop(0, n_blocks)
+    def _(b):
+        at = pl.ds(pl.multiple_of(b * fb, fb), fb)
+        lats = ids[:, at]
+        picks = chosen[...]
+        hit = jnp.zeros((tok, fb), jnp.bool_)
+        for k in range(picks.shape[1]):
+            hit = hit | (picks[:, k:k + 1] == lats)
+        active[:, at] = hit.astype(F32)
+
+    for zz in range(n_lat):
+        @pl.when(zz != z)
+        def _():
+            arrive(zz).wait_recv()
+            forward(zz, c).start()
+    for zz in range(n_lat):
+        @pl.when(zz != z)
+        def _():
+            forward(zz, 1 - c).wait_recv()
+
+    @pl.loop(0, n_blocks)
+    def _(b):
+        at = pl.ds(pl.multiple_of(b * fb, fb), fb)
+        wide_at = pl.ds(pl.multiple_of(b * fb * n_t, fb * n_t), fb * n_t)
+        pre = jnp.dot(feat[...], enc[:, at], preferred_element_type=F32)
+        code = (pre * active[:, at]).astype(BF)
+        codes[:, at] = code
+        rep = jnp.dot(code, spread[...], preferred_element_type=F32)
+        for t in range(n_t):
+            lhs[t * tok:(t + 1) * tok, wide_at] = jnp.where(target == t, rep, 0.0).astype(BF)
+
+    def decode_chunk(ch):
+        for j in range(GROUP):
+            loads[ch * GROUP + j].wait()
+        acc[...] = jnp.zeros_like(acc)
+
+        @pl.loop(0, n_blocks)
+        def _(b):
+            wide_at = pl.ds(pl.multiple_of(b * fb * n_t, fb * n_t), fb * n_t)
+            acc[...] += jnp.dot(lhs[:, wide_at], wide(xin, ch * GROUP, GROUP, b, fb),
+                                preferred_element_type=F32)
+
+        part[:, :, cols(ch)] = acc[...].astype(BF).reshape(n_t, tok, cw)
         for t in reversed(range(n_t)):
             @pl.when(t >= s)
             def _():
                 pair(ch, t).start()
-    for t in range(n_t):
-        @pl.when(t < s)
-        def _():
-            all_err[t] = jnp.zeros((2 * half, width), BF)
-    for ch in range(CHUNKS):
+
+    def add_pair(ch):
         for t in reversed(range(n_t)):
             @pl.when(t >= s)
             def _():
@@ -123,7 +223,8 @@
                 q[t, :, cols(ch)] = (part[t, mine, cols(ch)].astype(F32)
                                      + sib_rx[t, :, cols(ch)].astype(F32)).astype(BF)
                 to_target(ch, t).start()
-    for ch in range(CHUNKS):
+
+    def add_sources(ch):
         for ss in range(n_t):
             @pl.when(ss == s)
             def _():
@@ -137,7 +238,8 @@
             @pl.when(zz != z)
             def _():
                 to_lat(ch, zz).start()
-    for ch in range(CHUNKS):
+
+    def finish(ch):
         z_rx[z, :, cols(ch)] = zs[rblock(z), cols(ch)]
         for zz in range(n_lat):
             @pl.when(zz != z)
@@ -153,7 +255,8 @@
             @pl.when(zz != z)
             def _():
                 err_to_lat(ch, zz).start()
-    for ch in range(CHUNKS):
+
+    def spread_err(ch):
         for zz in range(n_lat):
             @pl.when(zz != z)
             def _():
@@ -163,13 +266,15 @@
             def _():
                 err_to_source(ch, ss).start()
         err_pair(ch, s).start()
-    for ch in range(CHUNKS):
+
+    def relay_err(ch):
         for t in range(n_t):
             @pl.when(t > s)
             def _():
                 err_from_target(ch, t).wait_recv()
                 err_pair(ch, t).start()
-    for ch in range(CHUNKS):
+
+    def drain(ch):
         for t in range(n_t):
             @pl.when(t >= s)
             def _():
@@ -190,34 +295,153 @@
                 to_lat(ch, zz).wait_send()
                 err_to_lat(ch, zz).wait_send()
 
-
-def exchange(part, targets):
-    n_t, tok, width = part.shape
+    stages = (decode_chunk, add_pair, add_sources, finish, spread_err, relay_err)
+    for step in range(chunks + len(stages) - 1):
+        for lag, stage in enumerate(stages):
+            if 0 <= step - lag < chunks:
+                stage(step - lag)
+    for ch in range(chunks):
+        drain(ch)
+    for zz in range(n_lat):
+        @pl.when(zz != z)
+        def _():
+            forward(zz, c).wait_send()
+            send(zz).wait_send()
+
+
+def forward_pass(inputs, targets, chosen, ids, enc, dec):
     n_lat = lax.axis_size("lat")
+    lat_dev, n_t, width = dec.shape
+    tok = inputs.shape[1]
     half = tok // 2
     rows = half // n_lat
+    fb = 256
+    chunks = width // (128 * GROUP)
     vm = pl.BlockSpec(memory_space=pltpu.VMEM)
     dma = pltpu.SemaphoreType.DMA
     sems = []
     for n in (n_t, n_t, n_lat, n_lat, n_t, n_t):
-        sems += [dma((CHUNKS, n)), dma((CHUNKS, n))]
+        sems += [dma((chunks, n)), dma((chunks, n))]
     return pl.pallas_call(
-        functools.partial(exchange_kernel, n_t, n_lat),
+        functools.partial(forward_kernel, n_t, n_lat),
         out_shape=(jax.ShapeDtypeStruct((rows, width), F32),
-                   jax.ShapeDtypeStruct((n_t, tok, width), BF)),
-        in_specs=[vm, vm],
-        out_specs=(vm, vm),
+                   jax.ShapeDtypeStruct((n_t, tok, width), BF),
+                   jax.ShapeDtypeStruct((tok, enc.shape[0]), BF),
+                   jax.ShapeDtypeStruct((tok, lat_dev), BF),
+                   jax.ShapeDtypeStruct((tok, lat_dev), F32)),
+        in_specs=[vm, vm, vm, vm, vm, pl.BlockSpec(memory_space=pl.ANY)],
+        out_specs=(vm, vm, vm, vm, vm),
         scratch_shapes=[
+            pltpu.VMEM((width // 128, lat_dev, n_t, 128), BF),
+            pltpu.VMEM((n_t * tok, lat_dev * n_t), BF),
+            pltpu.VMEM((fb, fb * n_t), BF),
+            pltpu.VMEM((n_t * tok, 128 * GROUP), F32),
+            pltpu.VMEM((n_t, tok, width), BF),
             pltpu.VMEM((n_t, half, width), BF),
             pltpu.VMEM((n_t, half, width), BF),
             pltpu.VMEM((n_t, half, width), BF),
             pltpu.VMEM((half, width), BF),
             pltpu.VMEM((n_lat, rows, width), BF),
-        ] + sems,
+            dma((width // 128,)),
+        ] + sems + [dma((n_lat,))] * 4,
         compiler_params=pltpu.CompilerParams(
-            collective_id=0, has_side_effects=True, vmem_limit_bytes=24 * 2**20),
-        cost_estimate=pl.CostEstimate(flops=2**24, bytes_accessed=2**24, transcendentals=0),
-    )(part, targets)
+            collective_id=0, has_side_effects=True, vmem_limit_bytes=56 * 2**20),
+        cost_estimate=pl.CostEstimate(
+            flops=10 * 10**9, bytes_accessed=2**24 + 2**22, transcendentals=0),
+    )(inputs, targets, chosen, ids, enc, dec)
+
+
+def grad_kernel(fb, n_blocks, feat, codes, active, err, dec, grad_enc, grad_dec,
+                xin, yout, gsum, lhs, spread, ebuf, sem, osem, esem):
+    tok = feat.shape[0]
+    rows_all, width = err.shape
+    n_t = rows_all // tok
+    for b in range(n_blocks):
+        for cp in load_copies(dec, xin, sem, b, fb):
+            cp.start()
+    spread[...] = spread_matrix(fb, n_t)
+    row_t = lax.broadcasted_iota(jnp.int32, (fb * n_t, tok), 0) % n_t
+    col_t = lax.broadcasted_iota(jnp.int32, (tok, fb * n_t), 1) % n_t
+    nt = (((1,), (1,)), ((), ()))
+    cw = 128 * GROUP
+    outs = []
+    for b in range(n_blocks):
+        cols = pl.ds(b * fb, fb)
+        rep = lax.dot_general(spread[...], codes[:, cols], (((0,), (1,)), ((), ())),
+                              preferred_element_type=F32)
+        for t in range(n_t):
+            lhs[:, t * tok:(t + 1) * tok] = jnp.where(row_t == t, rep, 0.0).astype(BF)
+
+        @pl.loop(0, width // cw)
+        def _(g):
+            at = pl.ds(pl.multiple_of(g * cw, cw), cw)
+            out = jnp.dot(lhs[...], err[:, at], preferred_element_type=F32).astype(BF)
+            for j in range(GROUP):
+                yout.at[g * GROUP + j, cols].reshape(fb * n_t, 128)[...] = (
+                    out[:, j * 128:(j + 1) * 128])
+
+        for j in range(width // 128):
+            cp = pltpu.make_async_copy(yout.at[j, cols],
+                                       grad_dec.at[cols, :, pl.ds(j * 128, 128)],
+                                       osem.at[b, j])
+            cp.start()
+            outs.append(cp)
+        for cp in load_copies(dec, xin, sem, b, fb):
+            cp.wait()
+        gsum[...] = jnp.zeros_like(gsum)
+
+        @pl.loop(0, width // cw)
+        def _(g):
+            at = pl.ds(pl.multiple_of(g * cw, cw), cw)
+            gsum[...] += lax.dot_general(err[:, at], wide(xin, g * GROUP, GROUP, b, fb), nt,
+                                         preferred_element_type=F32)
+
+        own = jnp.zeros((tok, fb * n_t), F32)
+        for t in range(n_t):
+            own = jnp.where(col_t == t, gsum[t * tok:(t + 1) * tok, :], own)
+        high = own.astype(BF)
+        low = (own - high.astype(F32)).astype(BF)
+        code_grad = (lax.dot_general(high, spread[...], nt, preferred_element_type=F32)
+                     + lax.dot_general(low, spread[...], nt, preferred_element_type=F32))
+        pre_grad = (code_grad * active[:, cols]).astype(BF)
+        ebuf[:, cols] = lax.dot_general(
+            feat[...], pre_grad, (((0,), (0,)), ((), ())), preferred_element_type=F32
+        ).astype(BF)
+        cp = pltpu.make_async_copy(ebuf.at[:, cols], grad_enc.at[:, cols], esem.at[b])
+        cp.start()
+        outs.append(cp)
+    for cp in outs:
+        cp.wait()
+
+
+def grads(features, codes, active, err, dec):
+    lat_dev, n_t, width = dec.shape
+    tok, d_in = features.shape
+    fb = 256
+    n_blocks = lat_dev // fb
+    vm = pl.BlockSpec(memory_space=pltpu.VMEM)
+    hbm = pl.BlockSpec(memory_space=pl.ANY)
+    tiles = pltpu.VMEM((width // 128, lat_dev, n_t, 128), BF)
+    return pl.pallas_call(
+        functools.partial(grad_kernel, fb, n_blocks),
+        out_shape=(jax.ShapeDtypeStruct((d_in, lat_dev), BF),
+                   jax.ShapeDtypeStruct((lat_dev, n_t, width), BF)),
+        in_specs=[vm, vm, vm, vm, hbm],
+        out_specs=(hbm, hbm),
+        scratch_shapes=[
+            tiles, tiles,
+            pltpu.VMEM((n_t * tok, fb * n_t), F32),
+            pltpu.VMEM((fb * n_t, n_t * tok), BF),
+            pltpu.VMEM((fb, fb * n_t), BF),
+            pltpu.VMEM((d_in, lat_dev), BF),
+            pltpu.SemaphoreType.DMA((n_blocks, width // 128)),
+            pltpu.SemaphoreType.DMA((n_blocks, width // 128)),
+            pltpu.SemaphoreType.DMA((n_blocks,)),
+        ],
+        compiler_params=pltpu.CompilerParams(vmem_limit_bytes=58 * 2**20),
+        cost_estimate=pl.CostEstimate(
+            flops=18 * 10**9, bytes_accessed=2**25 + 2**22, transcendentals=0),
+    )(features, codes, active, err, dec)
 
 
 def per_device(inputs, targets, top_index, enc_weight, dec_weight):
@@ -229,6 +453,17 @@
     per_layer = n_layer // layer_count
     layer_id = lax.axis_index("layer") // per_layer
     lat_first = (lax.axis_index("layer") % per_layer * n_lat + lax.axis_index("lat")) * lat_dev
+    tuned = (per_layer == 2 and layer_count == 4 and lat_dev % 256 == 0
+             and targets.shape[0] * 2 * n_lat == tok_count and targets.shape[0] % 16 == 0
+             and inputs.shape[2] % 256 == 0 and dec_weight.shape[2] % 512 == 0)
+    if tuned:
+        chosen = lax.dynamic_index_in_dim(top_index, layer_id, 0, keepdims=False)
+        ids = (lat_first + jnp.arange(lat_dev, dtype=jnp.int32))[None, :]
+        errors, err_used, features, codes, active = forward_pass(
+            inputs, targets, chosen, ids, enc_weight, dec_weight)
+        grad_enc, grad_dec = grads(
+            features, codes, active, err_used.reshape(-1, err_used.shape[2]), dec_weight)
+        return (errors, grad_enc, grad_dec)
     own_part = lax.dynamic_index_in_dim(inputs, layer_id, 0, keepdims=False)
     features = lax.all_gather(own_part, "lat", axis=1, tiled=True)
     preact = jnp.dot(features, enc_weight, preferred_element_type=jnp.float32)
@@ -240,20 +475,17 @@
     width = dec_weight.shape[2]
     row_count = targets.shape[0] * lax.axis_size(("layer", "lat"))
     result = jnp.einsum("nf,ftd->tnd", code_vals, dec_weight, preferred_element_type=jnp.float32)
-    if per_layer == 2 and targets.shape[0] * 2 * n_lat == tok_count and targets.shape[0] % 16 == 0:
-        errors, err_used = exchange(result.astype(BF), targets)
-    else:
-        result = result * reach_mask[:, None, None]
-        decoded = lax.psum_scatter(
-            result.reshape(row_count, width), ("layer", "lat"), scatter_dimension=0, tiled=True
-        )
-        errors = decoded - targets.astype(jnp.float32)
-        err_b = errors.astype(jnp.bfloat16)
-        all_err = lax.all_gather(err_b, ("layer", "lat"), axis=0, tiled=True)
-        err_used = (
-            all_err.reshape(layer_count, tok_count, width)
-            * reach_mask.astype(jnp.bfloat16)[:, None, None]
-        )
+    result = result * reach_mask[:, None, None]
+    decoded = lax.psum_scatter(
+        result.reshape(row_count, width), ("layer", "lat"), scatter_dimension=0, tiled=True
+    )
+    errors = decoded - targets.astype(jnp.float32)
+    err_b = errors.astype(jnp.bfloat16)
+    all_err = lax.all_gather(err_b, ("layer", "lat"), axis=0, tiled=True)
+    err_used = (
+        all_err.reshape(layer_count, tok_count, width)
+        * reach_mask.astype(jnp.bfloat16)[:, None, None]
+    )
     code_grad = jnp.einsum("lnd,fld->nf", err_used, dec_weight, preferred_element_type=jnp.float32)
     pre_grad = (code_grad * active).astype(jnp.bfloat16)
     grad_enc = lax.dot_general(

time: 148 us -> 96.3 us (0.65)
  matrix products: 61.1 us -> 0 us
  Pallas kernels: 39.3 us -> 93.2 us
  local copies, waits for them, and re-layouts: 24.7 us -> 1.68 us
  blocking collectives: 17.4 us -> 0 us
  other arithmetic: 4.7 us -> 0.6 us
    dot_general x5 -> x0, matrix products: 61.1 us -> none  [the longest x1 24.8 us: per_device(): jnp.einsum('nf,ftd->tnd', code_vals, dec_weight, preferred_element_type=j...]
    pallas_call x1 -> x2, Pallas kernels: 39.3 us -> 93.2 us  [the longest x1 56.9 us: forward_pass(): pl.pallas_call(functools.partial(forward_kernel, n_t, n_lat), out_shape=(...]
    unnamed x10 -> x5, local copies, waits for them, and re-layouts: 23.9 us -> 0.94 us
    all_gather x1 -> x0, blocking collectives: 17.4 us -> none  [per_device(): features = lax.all_gather(own_part, 'lat', axis=1, tiled=True)]
    reduce_or x1 -> x0, other arithmetic: 4.7 us -> none  [per_device(): jnp.any(chosen[:, :, None] == lat_ids[None, None, :], axis=1)]
where the time goes in v3:
time: 96.3 us; the launch traced here: 96.2 us
  Pallas kernels  93.2 us (97%)
  local copies, waits for them, and re-layouts  1.68 us (2%)
    pallas_call x1, Pallas kernels, forward_pass(): pl.pallas_call(functools.partial(forward_kernel, n_t, n_lat), out_shape=(...  56.9 us
    pallas_call x1, Pallas kernels, grads(): pl.pallas_call(functools.partial(grad_kernel, fb, n_blocks), out_shape=(j...  36.3 us

profile of v3, /device:TPU:0, one launch (start us, length us, event | category | flops | bytes accessed | tf_op | source)
XLA Modules:
  0.0 96.2 jit_solution(16719250489201525695)
XLA Ops:
  0.6 0.0 copy-start
  0.7 0.6 iota_add_fusion.ids
  1.3 0.3 copy-done
  1.5 0.7 copy.8
  2.3 56.9 %shard_map.76 = (f32[16,2048]{1,0:T(8,128)}, bf16[4,128,2048]{2,1,0:T(8,128)(2,1)}, bf16[128,2048]{1,0:T(8,128)(2,1)}, bf16[128,1024]{1,0:T(8,128)(2,1)}, f32[128,1024]{1,0:T(8,128)}) custom-call(bf16[4,128,512]{2,1,0:T(8,128)(2,1)} %own.1, bf16[16,2048]{1,0:T(8,128)(2,1)} %targets.1, s32[128,64]{1,0:T(8,128)} %bitcast.2, s32[1,1024]{1,0:T(1,128)} %iota_add_fusion.ids, ...), custom_call_target="tpu_custom_call" | custom-call | flops 10000000000 | bytes 20971520 | tf_op jit(solution)/shard_map/pallas_call | solution.py:325
  59.2 0.0 copy-start.1
  59.2 36.3 %shard_map.77 = (bf16[2048,1024]{1,0:T(8,128)(2,1)}, bf16[1024,4,2048]{2,1,0:T(4,128)(2,1)}) custom-call(bf16[128,2048]{1,0:T(8,128)(2,1)} %get-tuple-element.11.feat, bf16[128,1024]{1,0:T(8,128)(2,1)} %get-tuple-element.12.codes, f32[128,1024]{1,0:T(8,128)} %get-tuple-element.13.active, bf16[512,2048]{1,0:T(8,128)(2,1)} %bitcast.3, bf16[1024,4,2048]{2,1,0:T(4,128)(2,1)} %dec.3), custom_call_target="tpu_custom_call" | custom-call | flops 17999998976 | bytes 37748736 | tf_op jit(solution)/shard_map/pallas_call | solution.py:425
  95.5 0.0 copy-done.1
  95.5 0.7 copy.10
  (1 shorter events, 0.0 us)
Async XLA Ops:
  0.6 0.9 copy-start
  59.2 36.3 %copy-start.1 = (f32[16,2048]{1,0:T(8,128)S(1)}, f32[16,2048]{1,0:T(8,128)}, u32[]{:S(2)}) copy-start(f32[16,2048]{1,0:T(8,128)} %get-tuple-element.20) | copy-start | bytes 393220

commit v4 on v3

--- a/solution.py
+++ b/solution.py
@@ -32,6 +32,7 @@
 
 
 GROUP = 4
+CHUNK = 2
 
 
 def forward_kernel(n_t, n_lat, own, targets, chosen, ids, enc, dec,
@@ -45,7 +46,7 @@
     width = part.shape[2]
     half = part.shape[1] // 2
     rows = half // n_lat
-    cw = 128 * GROUP
+    cw = 128 * CHUNK
     chunks = width // cw
     fb = spread.shape[0]
     n_blocks = codes.shape[1] // fb
@@ -196,14 +197,14 @@
             lhs[t * tok:(t + 1) * tok, wide_at] = jnp.where(target == t, rep, 0.0).astype(BF)
 
     def decode_chunk(ch):
-        for j in range(GROUP):
-            loads[ch * GROUP + j].wait()
+        for j in range(CHUNK):
+            loads[ch * CHUNK + j].wait()
         acc[...] = jnp.zeros_like(acc)
 
         @pl.loop(0, n_blocks)
         def _(b):
             wide_at = pl.ds(pl.multiple_of(b * fb * n_t, fb * n_t), fb * n_t)
-            acc[...] += jnp.dot(lhs[:, wide_at], wide(xin, ch * GROUP, GROUP, b, fb),
+            acc[...] += jnp.dot(lhs[:, wide_at], wide(xin, ch * CHUNK, CHUNK, b, fb),
                                 preferred_element_type=F32)
 
         part[:, :, cols(ch)] = acc[...].astype(BF).reshape(n_t, tok, cw)
@@ -316,7 +317,7 @@
     half = tok // 2
     rows = half // n_lat
     fb = 256
-    chunks = width // (128 * GROUP)
+    chunks = width // (128 * CHUNK)
     vm = pl.BlockSpec(memory_space=pltpu.VMEM)
     dma = pltpu.SemaphoreType.DMA
     sems = []
@@ -335,7 +336,7 @@
             pltpu.VMEM((width // 128, lat_dev, n_t, 128), BF),
             pltpu.VMEM((n_t * tok, lat_dev * n_t), BF),
             pltpu.VMEM((fb, fb * n_t), BF),
-            pltpu.VMEM((n_t * tok, 128 * GROUP), F32),
+            pltpu.VMEM((n_t * tok, 128 * CHUNK), F32),
             pltpu.VMEM((n_t, tok, width), BF),
             pltpu.VMEM((n_t, half, width), BF),
             pltpu.VMEM((n_t, half, width), BF),

time: 96.3 us -> 104 us (1.080)
  Pallas kernels: 93.2 us -> 101 us
    pallas_call x1, Pallas kernels: 56.9 us -> 64.4 us  [forward_pass(): pl.pallas_call(functools.partial(forward_kernel, n_t, n_lat), out_shape=(...]
where the time goes in v4:
time: 104 us
  Pallas kernels  101 us (97%)
  local copies, waits for them, and re-layouts  1.68 us (2%)
    pallas_call x1, Pallas kernels, forward_pass(): pl.pallas_call(functools.partial(forward_kernel, n_t, n_lat), out_shape=(...  64.4 us
    pallas_call x1, Pallas kernels, grads(): pl.pallas_call(functools.partial(grad_kernel, fb, n_blocks), out_shape=(j...  36.4 us

profile of v4, /device:TPU:0, one launch (start us, length us, event | category | flops | bytes accessed | tf_op | source)
XLA Modules:
  0.0 103.8 jit_solution(11787027408701981716)
XLA Ops:
  0.6 0.0 copy-start
  0.7 0.6 iota_add_fusion.ids
  1.3 0.3 copy-done
  1.5 0.7 copy.8
  2.3 64.4 %shard_map.76 = (f32[16,2048]{1,0:T(8,128)}, bf16[4,128,2048]{2,1,0:T(8,128)(2,1)}, bf16[128,2048]{1,0:T(8,128)(2,1)}, bf16[128,1024]{1,0:T(8,128)(2,1)}, f32[128,1024]{1,0:T(8,128)}) custom-call(bf16[4,128,512]{2,1,0:T(8,128)(2,1)} %own.1, bf16[16,2048]{1,0:T(8,128)(2,1)} %targets.1, s32[128,64]{1,0:T(8,128)} %bitcast.2, s32[1,1024]{1,0:T(1,128)} %iota_add_fusion.ids, ...), custom_call_target="tpu_custom_call" | custom-call | flops 10000000000 | bytes 20971520 | tf_op jit(solution)/shard_map/pallas_call | solution.py:326
  66.7 0.0 copy-start.1
  66.7 36.4 %shard_map.77 = (bf16[2048,1024]{1,0:T(8,128)(2,1)}, bf16[1024,4,2048]{2,1,0:T(4,128)(2,1)}) custom-call(bf16[128,2048]{1,0:T(8,128)(2,1)} %get-tuple-element.11.feat, bf16[128,1024]{1,0:T(8,128)(2,1)} %get-tuple-element.12.codes, f32[128,1024]{1,0:T(8,128)} %get-tuple-element.13.active, bf16[512,2048]{1,0:T(8,128)(2,1)} %bitcast.3, bf16[1024,4,2048]{2,1,0:T(4,128)(2,1)} %dec.3), custom_call_target="tpu_custom_call" | custom-call | flops 17999998976 | bytes 37748736 | tf_op jit(solution)/shard_map/pallas_call | solution.py:426
  103.2 0.0 copy-done.1
  103.2 0.7 copy.10
  (1 shorter events, 0.0 us)
Async XLA Ops:
  0.6 0.9 copy-start
  66.7 36.5 %copy-start.1 = (f32[16,2048]{1,0:T(8,128)S(1)}, f32[16,2048]{1,0:T(8,128)}, u32[]{:S(2)}) copy-start(f32[16,2048]{1,0:T(8,128)} %get-tuple-element.20) | copy-start | bytes 393220
